TPU v7x, 32 devices: a whole 2x2x4 slice. The times are simulated.
32 devices in a mesh: groups: 2 (over x), pool: 4 (over y, core), tensor: 4 (over z).
Axes of the slice: x: 2, y: 2, z: 4, core: 2. Of those that a mesh axis runs over, the one named last changes fastest.
Arguments:
- hidden: bfloat16 [1024, 28672], P(('groups', 'pool'), 'tensor'), parts along dimension 0, may hold values from -6 to 6
- down_matrix: bfloat16 [28672, 8192], P('tensor', 'pool'), may hold values from -0.03125 to 0.03125
- adapter_shrink_weight: bfloat16 [16, 16, 28672], P('pool', None, 'tensor'), may hold values from -0.03125 to 0.03125
- adapter_expand_weight: bfloat16 [16, 16, 8192], P(None, None, 'pool'), may hold values from -1.5 to 1.5
- segment_adapter_id: int32 [64], P('groups'), parts along dimension 0, may hold values from 0 to 15
- adapter_storage_slot: int32 [16], replicated, may hold values from 0 to 15, each once
- segment_row_count: int32 [64], P('groups'), parts along dimension 0, may hold values from 1 to 16
Outputs:
- projected: bfloat16 [1024, 8192], P(('groups', 'tensor'), 'pool'), parts along dimension 0
There are 2 independent parts, one for each index of `groups`. A program takes and returns all parts, laid end to end along the dimension named above; an argument that names none is the same for every part. Nothing has to cross between parts.
All inputs are finite; a program needn't handle non-finite values.
Results may differ from a plain program's by a relative error of at most 0.001.
Values may be sent and summed in bfloat16 or wider, within the bound.
A program may use at most 128 MiB of HBM per device.

v0:
```python
import jax
import jax.numpy as jnp
from jax import lax
from jax.sharding import PartitionSpec as P

SEGMENT_ROWS = 16


adapter_scale = 2.0


def per_device(
    hidden,
    down_matrix,
    adapter_shrink_weight,
    adapter_expand_weight,
    segment_adapter_id,
    adapter_storage_slot,
    segment_row_count,
):
    gathered = lax.all_gather(hidden, "pool", axis=0, tiled=True)
    total_rows, ff_local = gathered.shape
    segments = total_rows // SEGMENT_ROWS
    base_output = jnp.dot(gathered, down_matrix, preferred_element_type=jnp.float32)
    adapter_ids = adapter_expand_weight.shape[0]
    same_id = segment_adapter_id[:, None] == jnp.arange(adapter_ids, dtype=jnp.int32)[None, :]
    storage_slot_index = jnp.sum(jnp.where(same_id, adapter_storage_slot[None, :], 0), axis=1)
    h_seg = gathered.reshape(segments, SEGMENT_ROWS, ff_local)
    every_adapter_id = lax.all_gather(adapter_shrink_weight, "pool", axis=0, tiled=True)
    chosen = jnp.take(every_adapter_id, storage_slot_index, axis=0)
    shrink = jnp.einsum("sgf,sqf->sgq", h_seg, chosen, preferred_element_type=jnp.float32)
    local_row_block = lax.psum_scatter(base_output, "tensor", scatter_dimension=0, tiled=True)
    local_segment_list = segments // lax.axis_size("tensor")
    first_seg = lax.axis_index("tensor") * local_segment_list
    whole_shrink = lax.psum(shrink, "tensor")
    own_shrink = lax.dynamic_slice_in_dim(whole_shrink, first_seg, local_segment_list, 0)
    owned_storage_slots = lax.dynamic_slice_in_dim(
        storage_slot_index, first_seg, local_segment_list, 0
    )
    owned_expand_weight = jnp.take(adapter_expand_weight, owned_storage_slots, axis=0).astype(
        jnp.float32
    )
    expand_output = jnp.einsum(
        "sgq,sqd->sgd", own_shrink, owned_expand_weight, precision=lax.Precision.HIGHEST
    )
    local_row_block = local_row_block + adapter_scale * expand_output.reshape(
        local_segment_list * SEGMENT_ROWS, -1
    )
    counts = lax.dynamic_slice_in_dim(segment_row_count, first_seg, local_segment_list, 0)
    valid_mask = (jnp.arange(SEGMENT_ROWS, dtype=jnp.int32)[None, :] < counts[:, None]).reshape(-1)
    return jnp.where(valid_mask[:, None], local_row_block, 0.0).astype(jnp.bfloat16)


def solution(mesh):
    in_specs = (
        P(("groups", "pool"), "tensor"),
        P("tensor", "pool"),
        P("pool", None, "tensor"),
        P(None, None, "pool"),
        P("groups"),
        P(),
        P("groups"),
    )
    out_specs = P(("groups", "tensor"), "pool")
    return jax.shard_map(
        per_device, mesh=mesh, in_specs=in_specs, out_specs=out_specs, check_vma=False
    )
```

profile of v0, /device:TPU:0, one launch (start us, length us, event | category | flops | bytes accessed | tf_op | source)
XLA Modules:
  0.0 193.3 jit_solution(16807863878740662136)
XLA Ops:
  6.5 0.0 copy-start
  6.5 0.0 all-gather.3.cloned.1.call-start
  6.5 0.7 all-gather.3.cloned.1.call-update
  7.3 0.0 all-gather.5.cloned.1.call-start
  7.3 0.7 all-gather.5.cloned.1.call-update
  8.0 0.0 copy-start.1
  8.0 0.0 copy-start.2
  8.0 0.0 copy-start.3
  8.0 0.0 reduce-scatter.2.cloned.1.call-start
  8.1 55.9 %all-gather.3.cloned.1.call-done = bf16[512,7168]{1,0:T(8,128)(2,1)} async-done(((bf16[128,7168]{1,0:T(8,128)(2,1)}), bf16[512,7168]{1,0:T(8,128)(2,1)}) %all-gather.3.cloned.1.call-update) | async-done | bytes 7340048 | tf_op jit(solution)/shard_map/all_gather | solution.py:21
  64.0 22.0 %fusion.17 = f32[512,2048]{1,0:T(8,128)} fusion(bf16[512,7168]{1,0:T(8,128)(2,1)} %all-gather.3.cloned.1.call-done, bf16[7168,2048]{1,0:T(8,128)(2,1)} %param.8), kind=kOutput, calls=%fused_computation.29 | convolution fusion | flops 15032385536 | bytes 40894464 | tf_op jit(solution)/shard_map/dot_general | solution.py:24
  86.0 0.0 reduce-scatter.2.cloned.1.call-update
  86.0 0.0 copy-done.1
  86.0 0.1 dynamic_slice.9
  86.1 0.1 iota_compare_fusion.1
  86.1 0.1 lt.54
  86.2 0.0 copy-done.2
  86.2 0.0 copy-done.3
  86.3 0.1 select_reduce_fusion
  86.3 0.1 compare_and_fusion
  86.4 0.0 copy-done
  86.4 0.6 gather_fusion.1
  87.1 10.0 %all-gather.5.cloned.1.call-done = bf16[16,16,7168]{2,1,0:T(8,128)(2,1)} async-done(((bf16[4,16,7168]{2,1,0:T(8,128)(2,1)}), bf16[16,16,7168]{2,1,0:T(8,128)(2,1)}) %all-gather.5.cloned.1.call-update) | async-done | bytes 3670032 | tf_op jit(solution)/shard_map/all_gather | solution.py:29
  97.1 6.1 %gather_fusion = bf16[32,16,7168]{2,1,0:T(8,128)(2,1)} fusion(bf16[16,16,7168]{2,1,0:T(8,128)(2,1)} %all-gather.5.cloned.1.call-done, s32[1024]{0:T(1024)S(1)} %pad_clamp_fusion.1), kind=kCustom, calls=%fused_computation | custom fusion | bytes 14680192 | tf_op jit(solution)/shard_map/jit(_take)/gather | solution.py:30
  103.2 9.5 %fusion.4 = f32[32,16,16]{1,2,0:T(8,128)S(1)} fusion(bf16[32,16,7168]{2,1,0:T(8,128)(2,1)} %bitcast.16, bf16[32,16,7168]{2,1,0:T(8,128)(2,1)} %gather_fusion, pred[32]{0:T(512)(128)(4,1)S(1)} %compare_and_fusion.1), kind=kOutput, calls=%fused_computation.7 | convolution fusion | flops 121110528 | bytes 14712864 | tf_op jit(solution)/shard_map/sgf,sqf->sgq/dot_general | solution.py:31
  112.7 33.4 %psum.7 = f32[32,16,16]{1,2,0:T(8,128)S(1)} all-reduce(f32[32,16,16]{1,2,0:T(8,128)S(1)} %fusion.4), channel_id=1, replica_groups=mesh['groups'=2,'pool'=4,'tensor'=4] {'tensor'}, use_global_device_ids=true, to_apply=%region_2.3 | all-reduce | flops 8192 | bytes 65536 | tf_op jit(solution)/shard_map/psum | solution.py:35
  146.0 0.6 convolution_multiply_fusion
  146.7 37.9 %reduce-scatter.2.cloned.1.call-done = f32[128,2048]{1,0:T(8,128)} async-done(((f32[512,2048]{1,0:T(8,128)}), f32[128,2048]{1,0:T(8,128)}) %reduce-scatter.2.cloned.1.call-update) | async-done | bytes 1048592 | tf_op jit(solution)/shard_map/reduce_scatter | solution.py:32
  184.6 2.2 %fusion.8 = bf16[128,2048]{1,0:T(8,128)(2,1)} fusion(f32[128,2048]{1,0:T(8,128)} %reduce-scatter.2.cloned.1.call-done, f32[8,16,2048]{2,1,0:T(8,128)S(1)} %convolution_multiply_fusion, pred[128]{0:T(512)(128)(4,1)S(1)} %lt.54), kind=kLoop, calls=%fused_computation.10 | loop fusion | flops 786432 | bytes 2621568 | tf_op jit(solution)/shard_map/convert_element_type | solution.py:51
  (4 shorter events, 0.0 us)
Async XLA Ops:
  6.5 79.9 %copy-start = (bf16[16,16,2048]{2,1,0:T(8,128)(2,1)S(1)}, bf16[16,16,2048]{2,1,0:T(8,128)(2,1)}, u32[]{:S(2)}) copy-start(bf16[16,16,2048]{2,1,0:T(8,128)(2,1)} %param.10) | copy-start | bytes 3145732
  6.5 57.5 %all-gather.3.cloned.1.call-start = ((), (), s32[]{:S(2)}) async-start(), calls=%async_computation.1 | async-start | bytes 9175040 | tf_op jit(solution)/shard_map/all_gather | solution.py:21
  7.3 89.8 %all-gather.5.cloned.1.call-start = ((), (), s32[]{:S(2)}) async-start(), calls=%async_computation.3 | async-start | bytes 4587520 | tf_op jit(solution)/shard_map/all_gather | solution.py:29
  8.0 78.0 %copy-start.1 = (s32[32]{0:T(128)S(1)}, s32[32]{0:T(128)}, u32[]{:S(2)}) copy-start(s32[32]{0:T(128)} %param.13) | copy-start | bytes 388
  8.0 78.2 %copy-start.2 = (s32[16]{0:T(128)S(1)}, s32[16]{0:T(128)}, u32[]{:S(2)}) copy-start(s32[16]{0:T(128)} %param.12) | copy-start | bytes 196
  8.0 78.2 %copy-start.3 = (s32[32]{0:T(128)S(1)}, s32[32]{0:T(128)}, u32[]{:S(2)}) copy-start(s32[32]{0:T(128)} %param.11) | copy-start | bytes 388
  8.0 176.6 %reduce-scatter.2.cloned.1.call-start = ((), (), s32[]{:S(2)}) async-start(), calls=%async_computation.2 | async-start | bytes 5242880 | tf_op jit(solution)/shard_map/reduce_scatter | solution.py:32
Sparse Core Ops, SparseCore 0:
  8.9 55.0 all-gather.2
  65.5 31.4 all-gather.4
  99.4 85.1 reduce-scatter.1
where the time goes:
time: 194 us; the launch traced here: 193 us
  waiting for transfers between devices  105 us (54%)
  blocking collectives  33.4 us (17%)
  matrix products  32.1 us (17%)
  between operations  13.2 us (7%)
  local copies, waits for them, and re-layouts  6.83 us (4%)
  other arithmetic  2.46 us (1%)
    all_gather x1, waiting for transfers between devices, per_device(): gathered = lax.all_gather(hidden, 'pool', axis=0, tiled=True)  55.9 us
    reduce_scatter x1, waiting for transfers between devices, per_device(): lax.psum_scatter(base_output, 'tensor', scatter_dimension=0, tiled=True)  37.9 us
    psum x1, blocking collectives, per_device(): whole_shrink = lax.psum(shrink, 'tensor')  33.4 us
    dot_general x1, matrix products, per_device(): jnp.dot(gathered, down_matrix, preferred_element_type=jnp.float32)  22 us
    all_gather x1, waiting for transfers between devices, per_device(): lax.all_gather(adapter_shrink_weight, 'pool', axis=0, tiled=True)  10 us
    dot_general x1, matrix products, per_device(): jnp.einsum('sgf,sqf->sgq', h_seg, chosen, preferred_element_type=jnp.floa...  9.5 us
    gather x1, local copies, waits for them, and re-layouts, per_device(): chosen = jnp.take(every_adapter_id, storage_slot_index, axis=0)  6.07 us
  transfers between devices with their start and end apart: 3, of which 3 were waited for; matrix products, arithmetic and copies ran while one was open for 20% of the time, Pallas kernels for 0%

commit v1 on v0

--- a/solution.py
+++ b/solution.py
@@ -1,6 +1,8 @@
 import jax
 import jax.numpy as jnp
 from jax import lax
+from jax.experimental import pallas as pl
+from jax.experimental.pallas import tpu as pltpu
 from jax.sharding import PartitionSpec as P
 
 SEGMENT_ROWS = 16
@@ -51,6 +53,334 @@
     return jnp.where(valid_mask[:, None], local_row_block, 0.0).astype(jnp.bfloat16)
 
 
+MESH = pl.DeviceIdType.MESH
+LEVELS = 32500.0
+TILES = 4
+VMEM_LIMIT = 60 * 2**20
+CHUNKS = 4
+
+
+def fused_kernel(
+    id_ref, slot_ref, count_ref, hidden_ref, down_ref, shrink_ref, expand_ref, out_ref,
+    h, w, a, e, acc, q_send, q_recv, s_send, s_recv, r_send, r_recv,
+    w_sem, load_sem, y_send_sem, y_recv_sem, c_send_sem, c_recv_sem, f_send_sem, f_recv_sem,
+    q_send_sem, q_recv_sem, s_send_sem, s_recv_sem, r_send_sem, r_recv_sem,
+):
+    pools, steps = lax.axis_size("pool"), lax.axis_size("tensor")
+    g, p, z = lax.axis_index("groups"), lax.axis_index("pool"), lax.axis_index("tensor")
+    y, c = p // 2, p % 2
+    core_peer = y * 2 + (1 - c)
+    y_peer = (1 - y) * 2 + c
+    block, ff = h.shape[1], h.shape[2]
+    tile = w.shape[2]
+    part = block // CHUNKS
+    rank = r_send.shape[1]
+    owned = a.shape[0] // rank
+
+    def remote(src, dst, send, recv, pool, step):
+        return pltpu.make_async_remote_copy(
+            src_ref=src, dst_ref=dst, send_sem=send, recv_sem=recv,
+            device_id=(g, pool, step), device_id_type=MESH,
+        )
+
+    def w_copy(n):
+        return pltpu.make_async_copy(
+            down_ref.at[:, pl.ds(pl.multiple_of(n * tile, tile), tile)], w.at[n], w_sem.at[n]
+        )
+
+    own_load = pltpu.make_async_copy(hidden_ref, h.at[p], load_sem.at[0])
+    a_load = pltpu.make_async_copy(shrink_ref, a, load_sem.at[1])
+    e_load = pltpu.make_async_copy(expand_ref, e, load_sem.at[2])
+    own_load.start()
+    for n in range(TILES):
+        w_copy(n).start()
+
+    barrier = pltpu.get_barrier_semaphore()
+    for i in range(1, pools * steps):
+        other = (p * steps + z + i) % (pools * steps)
+        pl.semaphore_signal(
+            barrier, inc=1, device_id=(g, other // steps, other % steps), device_id_type=MESH
+        )
+    pl.semaphore_wait(barrier, pools * steps - 1)
+
+    def y_copy(k, blk):
+        rows = pl.ds(pl.multiple_of(k * part, part), part)
+        return remote(
+            hidden_ref.at[rows], h.at[blk, rows], y_send_sem.at[k], y_recv_sem.at[k], y_peer, z
+        )
+
+    def fwd_copy(k, blk):
+        rows = pl.ds(pl.multiple_of(k * part, part), part)
+        return remote(
+            h.at[blk, rows], h.at[blk, rows], f_send_sem.at[k], f_recv_sem.at[k], core_peer, z
+        )
+
+    def core_copy(blk):
+        return remote(hidden_ref, h.at[blk], c_send_sem.at[0], c_recv_sem.at[0], core_peer, z)
+
+    y_copy(0, p).start()
+    core_copy(p).start()
+    for k in range(1, CHUNKS):
+        y_copy(k, p).start()
+    a_load.start()
+    e_load.start()
+
+    def emit(x, n, blk, first, rows, scales):
+        top = jnp.max(jnp.abs(x), axis=1, keepdims=True)
+        scale = (jnp.maximum(top, 1e-30) * (1.0 / LEVELS)).astype(jnp.bfloat16).astype(jnp.float32)
+        coded = jnp.round(x * (1.0 / scale)).astype(jnp.int32).astype(jnp.int16)
+        cols = pl.ds(pl.multiple_of(n * tile, tile), tile)
+        here = pl.ds(pl.multiple_of(first, 16), rows)
+
+        @pl.when(blk == z)
+        def _():
+            acc[here, cols] = x
+
+        @pl.when(blk != z)
+        def _():
+            q_send[blk, here, cols] = coded
+            remote(
+                q_send.at[blk, here, cols], q_recv.at[z, here, cols],
+                q_send_sem.at[blk], q_recv_sem.at[z], p, blk,
+            ).start()
+
+        lane = lax.broadcasted_iota(jnp.int32, scales.shape, 1)
+        return jnp.where(lane == n, scale, scales)
+
+    def emit_scales(scales, blk, first, rows):
+        here = pl.ds(pl.multiple_of(first, 16), rows)
+
+        @pl.when(blk != z)
+        def _():
+            s_send[blk, here] = scales.astype(jnp.bfloat16)
+            remote(
+                s_send.at[blk, here], s_recv.at[z, here],
+                s_send_sem.at[blk], s_recv_sem.at[z], p, blk,
+            ).start()
+
+    def slots_of(blk):
+        per = block // SEGMENT_ROWS
+        lane = lax.broadcasted_iota(jnp.int32, (1, block), 1)
+        vec = jnp.zeros((1, block), jnp.int32)
+        for i in range(per):
+            vec = jnp.where(lane >= i * SEGMENT_ROWS, slot_ref[id_ref[blk * per + i]], vec)
+        return vec
+
+    def shrink_block(blk):
+        s = lax.dot_general(
+            a[...], h[blk], (((1,), (1,)), ((), ())), preferred_element_type=jnp.float32
+        )
+        row_slot = lax.broadcasted_iota(jnp.int32, s.shape, 0) // rank + owned * p
+        s = jnp.where(row_slot == slots_of(blk), s, 0.0)
+        total = s[0:rank]
+        for i in range(1, owned):
+            total = total + s[i * rank:(i + 1) * rank]
+        r_send[blk] = total
+        me = p * steps + z
+
+        @pl.when(blk == z)
+        def _():
+            r_recv[me] = total
+
+        for i in range(pools):
+            @pl.when(jnp.logical_or(blk != z, p != i))
+            def _():
+                remote(
+                    r_send.at[blk], r_recv.at[me],
+                    r_send_sem.at[blk * pools + i], r_recv_sem.at[me], i, blk,
+                ).start()
+
+    own_load.wait()
+    remote(
+        hidden_ref, h.at[core_peer], c_send_sem.at[0], c_recv_sem.at[0], core_peer, z
+    ).wait_recv()
+
+    def near(n, scales):
+        w_copy(n).wait()
+        lhs = jnp.concatenate([h[y * 2], h[y * 2 + 1]], axis=0)
+        x = jnp.dot(lhs, w[n], preferred_element_type=jnp.float32)
+        return tuple(
+            emit(x[j * block:(j + 1) * block], n, y * 2 + j, 0, block, scales[j]) for j in range(2)
+        )
+
+    zero = jnp.zeros((block, 128), jnp.float32)
+    scales = lax.fori_loop(0, TILES, near, (zero, zero))
+    for j in range(2):
+        emit_scales(scales[j], y * 2 + j, 0, block)
+
+    a_load.wait()
+
+    def near_shrink(j, _):
+        shrink_block(y * 2 + j)
+        return 0
+
+    lax.fori_loop(0, 2, near_shrink, 0)
+
+    def far(k, _):
+        y_copy(k, y_peer).wait_recv()
+        fwd_copy(k, y_peer).start()
+        far_first = (1 - y) * 2
+        fwd_copy(k, far_first + (1 - c)).wait_recv()
+        first = pl.multiple_of(k * part, part)
+        rows = pl.ds(first, part)
+
+        def body(n, scales):
+            lhs = jnp.concatenate([h[far_first, rows], h[far_first + 1, rows]], axis=0)
+            x = jnp.dot(lhs, w[n], preferred_element_type=jnp.float32)
+            return tuple(
+                emit(x[j * part:(j + 1) * part], n, far_first + j, first, part, scales[j])
+                for j in range(2)
+            )
+
+        zero = jnp.zeros((part, 128), jnp.float32)
+        scales = lax.fori_loop(0, TILES, body, (zero, zero))
+        for j in range(2):
+            emit_scales(scales[j], far_first + j, first, part)
+        return 0
+
+    lax.fori_loop(0, CHUNKS, far, 0)
+
+    def far_shrink(j, _):
+        shrink_block((1 - y) * 2 + j)
+        return 0
+
+    lax.fori_loop(0, 2, far_shrink, 0)
+
+    me = p * steps + z
+    e_load.wait()
+    for i in range(pools * steps):
+        @pl.when(me != i)
+        def _():
+            remote(
+                r_recv.at[i], r_recv.at[i], r_send_sem.at[i], r_recv_sem.at[i], p, z
+            ).wait_recv()
+    whole = r_recv[0]
+    for i in range(1, pools * steps):
+        whole = whole + r_recv[i]
+    adapters = e.shape[0] // rank
+    spread = jnp.concatenate([whole] * adapters, axis=0)
+    row_slot = lax.broadcasted_iota(jnp.int32, spread.shape, 0) // rank
+    spread = jnp.where(row_slot == slots_of(z), spread, 0.0).T
+    hi = spread.astype(jnp.bfloat16)
+    rest = spread - hi.astype(jnp.float32)
+    mid = rest.astype(jnp.bfloat16)
+    low = (rest - mid.astype(jnp.float32)).astype(jnp.bfloat16)
+    for n in range(TILES):
+        cols = slice(n * tile, (n + 1) * tile)
+        add = jnp.dot(hi, e[:, cols], preferred_element_type=jnp.float32)
+        add += jnp.dot(mid, e[:, cols], preferred_element_type=jnp.float32)
+        add += jnp.dot(low, e[:, cols], preferred_element_type=jnp.float32)
+        acc[:, cols] = acc[:, cols] + adapter_scale * add
+
+    per = block // SEGMENT_ROWS
+    row = lax.broadcasted_iota(jnp.int32, (block, 1), 0)
+    live = jnp.zeros((block, 1), jnp.int32)
+    for i in range(per):
+        live = jnp.where(row >= i * SEGMENT_ROWS, count_ref[z * per + i] + i * SEGMENT_ROWS, live)
+    for i in range(1, steps):
+        src = (z + i) % steps
+        remote(
+            q_recv.at[src], q_recv.at[src], q_send_sem.at[src], q_recv_sem.at[src], p, z
+        ).wait_recv()
+        remote(
+            s_recv.at[src], s_recv.at[src], s_send_sem.at[src], s_recv_sem.at[src], p, z
+        ).wait_recv()
+    for n in range(TILES):
+        cols = slice(n * tile, (n + 1) * tile)
+        x = acc[:, cols]
+        for i in range(1, steps):
+            src = (z + i) % steps
+            scale = s_recv[src].astype(jnp.float32)[:, n:n + 1]
+            x = x + q_recv[src, :, cols].astype(jnp.int32).astype(jnp.float32) * scale
+        out_ref[:, cols] = jnp.where(row < live, x, 0.0).astype(jnp.bfloat16)
+
+    core_copy(p).wait_send()
+    for k in range(CHUNKS):
+        y_copy(k, p).wait_send()
+        fwd_copy(k, y_peer).wait_send()
+    for i in range(1, steps):
+        blk = (z + i) % steps
+        remote(
+            q_send.at[blk], q_recv.at[z], q_send_sem.at[blk], q_recv_sem.at[z], p, blk
+        ).wait_send()
+        remote(
+            s_send.at[blk], s_recv.at[z], s_send_sem.at[blk], s_recv_sem.at[z], p, blk
+        ).wait_send()
+    for t in range(steps):
+        for i in range(pools):
+            @pl.when(jnp.logical_or(z != t, p != i))
+            def _():
+                remote(
+                    r_send.at[t], r_recv.at[me], r_send_sem.at[t * pools + i], r_recv_sem.at[me],
+                    i, t,
+                ).wait_send()
+
+
+def fused_device(
+    hidden,
+    down_matrix,
+    adapter_shrink_weight,
+    adapter_expand_weight,
+    segment_adapter_id,
+    adapter_storage_slot,
+    segment_row_count,
+):
+    pools, steps = lax.axis_size("pool"), lax.axis_size("tensor")
+    block, ff = hidden.shape
+    width = down_matrix.shape[1]
+    owned, rank, _ = adapter_shrink_weight.shape
+    adapters = adapter_expand_weight.shape[0]
+    a = adapter_shrink_weight.reshape(owned * rank, ff)
+    e = adapter_expand_weight.reshape(adapters * rank, width)
+    f32, bf16 = jnp.float32, jnp.bfloat16
+    dma = pltpu.SemaphoreType.DMA
+    smem = pl.BlockSpec(memory_space=pltpu.SMEM)
+    hbm = pl.BlockSpec(memory_space=pl.ANY)
+    return pl.pallas_call(
+        fused_kernel,
+        out_shape=jax.ShapeDtypeStruct((block, width), bf16),
+        in_specs=[smem] * 3 + [hbm] * 4,
+        out_specs=pl.BlockSpec(memory_space=pltpu.VMEM),
+        scratch_shapes=[
+            pltpu.VMEM((pools, block, ff), bf16),
+            pltpu.VMEM((TILES, ff, width // TILES), bf16),
+            pltpu.VMEM((owned * rank, ff), bf16),
+            pltpu.VMEM((adapters * rank, width), bf16),
+            pltpu.VMEM((block, width), f32),
+            pltpu.VMEM((steps, block, width), jnp.int16),
+            pltpu.VMEM((steps, block, width), jnp.int16),
+            pltpu.VMEM((steps, block, 128), bf16),
+            pltpu.VMEM((steps, block, 128), bf16),
+            pltpu.VMEM((steps, rank, block), f32),
+            pltpu.VMEM((pools * steps, rank, block), f32),
+            dma((TILES,)), dma((3,)), dma((CHUNKS,)), dma((CHUNKS,)), dma((1,)), dma((1,)),
+            dma((CHUNKS,)), dma((CHUNKS,)), dma((steps,)), dma((steps,)), dma((steps,)),
+            dma((steps,)), dma((pools * steps,)), dma((pools * steps,)),
+        ],
+        compiler_params=pltpu.CompilerParams(
+            collective_id=0, has_side_effects=True, vmem_limit_bytes=VMEM_LIMIT
+        ),
+        cost_estimate=pl.CostEstimate(
+            flops=2 * pools * block * ff * width, bytes_accessed=2 * ff * width, transcendentals=0
+        ),
+    )(segment_adapter_id, adapter_storage_slot, segment_row_count, hidden, down_matrix, a, e)
+
+
+def fits(mesh, shapes):
+    hidden, down = shapes
+    parts = mesh.shape["groups"] * mesh.shape["pool"]
+    rows = hidden[0] // parts
+    ff, width = down[0] // mesh.shape["tensor"], down[1] // mesh.shape["pool"]
+    return (
+        mesh.shape["pool"] == 4
+        and mesh.shape["tensor"] == 4
+        and rows == 128
+        and width % (128 * TILES) == 0
+        and ff % 128 == 0
+        and 2 * ff * (width + 4 * rows) < 40 * 2**20
+    )
+
+
 def solution(mesh):
     in_specs = (
         P(("groups", "pool"), "tensor"),
@@ -62,6 +392,11 @@
         P("groups"),
     )
     out_specs = P(("groups", "tensor"), "pool")
-    return jax.shard_map(
-        per_device, mesh=mesh, in_specs=in_specs, out_specs=out_specs, check_vma=False
-    )
+
+    def run(*args):
+        body = fused_device if fits(mesh, (args[0].shape, args[1].shape)) else per_device
+        return jax.shard_map(
+            body, mesh=mesh, in_specs=in_specs, out_specs=out_specs, check_vma=False
+        )(*args)
+
+    return run

time: 194 us -> 84.4 us (0.44)
  waiting for transfers between devices: 105 us -> 0 us
  Pallas kernels: 0 us -> 82.4 us
  blocking collectives: 33.4 us -> 0 us
  matrix products: 32.1 us -> 0 us
  between operations: 13.2 us -> 0.01 us
  local copies, waits for them, and re-layouts: 6.83 us -> 1.88 us
  other arithmetic: 2.46 us -> 0 us
    pallas_call x0 -> x1, Pallas kernels: none -> 82.4 us  [fused_device(): pl.pallas_call(fused_kernel, out_shape=jax.ShapeDtypeStruct((block, width...]
    all_gather x2 -> x0, waiting for transfers between devices: 65.9 us -> none  [the longest x1 55.9 us: per_device(): gathered = lax.all_gather(hidden, 'pool', axis=0, tiled=True)]
    reduce_scatter x1 -> x0, waiting for transfers between devices: 37.9 us -> none  [per_device(): lax.psum_scatter(base_output, 'tensor', scatter_dimension=0, tiled=True)]
    psum x1 -> x0, blocking collectives: 33.4 us -> none  [per_device(): whole_shrink = lax.psum(shrink, 'tensor')]
    dot_general x3 -> x0, matrix products: 32.1 us -> none  [the longest x1 22 us: per_device(): jnp.dot(gathered, down_matrix, preferred_element_type=jnp.float32)]
    gather x2 -> x0, local copies, waits for them, and re-layouts: 6.65 us -> none  [the longest x1 6.07 us: per_device(): chosen = jnp.take(every_adapter_id, storage_slot_index, axis=0)]
    convert_element_type x1 -> x0, other arithmetic: 2.19 us -> none  [per_device(): jnp.where(valid_mask[:, None], local_row_block, 0.0).astype(jnp.bfloat16)]
  transfers between devices with their start and end apart: 3 -> 0, of which waited for: 3 -> 0; matrix products, arithmetic and copies ran while one was open for 20% -> 0% of each run, Pallas kernels for 0% -> 0%
where the time goes in v1:
time: 84.4 us; the launch traced here: 84.3 us
  Pallas kernels  82.4 us (98%)
  local copies, waits for them, and re-layouts  1.88 us (2%)
    pallas_call x1, Pallas kernels, fused_device(): pl.pallas_call(fused_kernel, out_shape=jax.ShapeDtypeStruct((block, width...  82.4 us
    unnamed x1, local copies, waits for them, and re-layouts  1.88 us

profile of v1, /device:TPU:0, one launch (start us, length us, event | category | flops | bytes accessed | tf_op | source)
XLA Modules:
  0.0 84.3 jit_solution(7596128227012462663)
XLA Ops:
  0.0 82.4 %shard_map.73 = bf16[128,2048]{1,0:T(8,128)(2,1)} custom-call(s32[32]{0:T(128)} %id_ref.1, s32[16]{0:T(128)} %slot_ref.1, s32[32]{0:T(128)} %count_ref.1, bf16[128,7168]{1,0:T(8,128)(2,1)} %hidden_ref.1, bf16[7168,2048]{1,0:T(8,128)(2,1)} %down_ref.1, bf16[64,7168]{1,0:T(8,128)(2,1)} %bitcast.3, bf16[256,2048]{1,0:T(8,128)(2,1)} %bitcast.2), custom_call_target="tpu_custom_call" | custom-call | flops 15032385536 | bytes 29360128 | tf_op jit(solution)/shard_map/pallas_call | solution.py:339
  82.4 1.9 %copy.9 = bf16[128,2048]{1,0:T(8,128)(2,1)} copy(bf16[128,2048]{1,0:T(8,128)(2,1)} %shard_map.73) | data formatting | bytes 1048576

commit v2 on v1

--- a/solution.py
+++ b/solution.py
@@ -57,14 +57,16 @@
 LEVELS = 32500.0
 TILES = 4
 VMEM_LIMIT = 60 * 2**20
-CHUNKS = 4
+PIECES = 8
+NEAR = (4, 4)
+FAR = (2, 3, 2, 1)
 
 
 def fused_kernel(
     id_ref, slot_ref, count_ref, hidden_ref, down_ref, shrink_ref, expand_ref, out_ref,
-    h, w, a, e, acc, q_send, q_recv, s_send, s_recv, r_send, r_recv,
+    h, w, a, e, acc, stash, q_send, q_recv, s_send, s_recv, m_recv, ms_recv, r_send, r_recv,
     w_sem, load_sem, y_send_sem, y_recv_sem, c_send_sem, c_recv_sem, f_send_sem, f_recv_sem,
-    q_send_sem, q_recv_sem, s_send_sem, s_recv_sem, r_send_sem, r_recv_sem,
+    q_send_sem, q_recv_sem, s_send_sem, s_recv_sem, m_recv_sem, ms_recv_sem, r_send_sem, r_recv_sem,
 ):
     pools, steps = lax.axis_size("pool"), lax.axis_size("tensor")
     g, p, z = lax.axis_index("groups"), lax.axis_index("pool"), lax.axis_index("tensor")
@@ -73,7 +75,7 @@
     y_peer = (1 - y) * 2 + c
     block, ff = h.shape[1], h.shape[2]
     tile = w.shape[2]
-    part = block // CHUNKS
+    part = block // PIECES
     rank = r_send.shape[1]
     owned = a.shape[0] // rank
 
@@ -120,43 +122,117 @@
 
     y_copy(0, p).start()
     core_copy(p).start()
-    for k in range(1, CHUNKS):
+    for k in range(1, PIECES):
         y_copy(k, p).start()
     a_load.start()
     e_load.start()
 
-    def emit(x, n, blk, first, rows, scales):
+    def inner(half):
+        return 2 - half
+
+    def code(x, n, scales):
         top = jnp.max(jnp.abs(x), axis=1, keepdims=True)
         scale = (jnp.maximum(top, 1e-30) * (1.0 / LEVELS)).astype(jnp.bfloat16).astype(jnp.float32)
         coded = jnp.round(x * (1.0 / scale)).astype(jnp.int32).astype(jnp.int16)
-        cols = pl.ds(pl.multiple_of(n * tile, tile), tile)
-        here = pl.ds(pl.multiple_of(first, 16), rows)
-
-        @pl.when(blk == z)
+        lane = lax.broadcasted_iota(jnp.int32, scales.shape, 1)
+        return coded, jnp.where(lane == n, scale, scales)
+
+    def decode(coded, slab, n):
+        return coded.astype(jnp.int32).astype(jnp.float32) * slab.astype(jnp.float32)[:, n:n + 1]
+
+    def post(blk, half, j, u, here, cols, scale_send):
+        q, ready, to_own, own_sem, to_inner, inner_sem = (
+            (s_send, s_send_sem, s_recv, s_recv_sem, ms_recv, ms_recv_sem)
+            if scale_send
+            else (q_send, q_send_sem, q_recv, q_recv_sem, m_recv, m_recv_sem)
+        )
+
+        @pl.when(z // 2 == half)
         def _():
-            acc[here, cols] = x
-
-        @pl.when(blk != z)
+            remote(
+                q.at[blk, here, cols], to_own.at[0, here, cols],
+                ready.at[blk], own_sem.at[0], p, blk,
+            ).start()
+
+        @pl.when(z // 2 != half)
         def _():
-            q_send[blk, here, cols] = coded
             remote(
-                q_send.at[blk, here, cols], q_recv.at[z, here, cols],
-                q_send_sem.at[blk], q_recv_sem.at[z], p, blk,
+                q.at[blk, here, cols], to_inner.at[j, here, cols],
+                ready.at[blk], inner_sem.at[u], p, inner(half),
             ).start()
 
-        lane = lax.broadcasted_iota(jnp.int32, scales.shape, 1)
-        return jnp.where(lane == n, scale, scales)
-
-    def emit_scales(scales, blk, first, rows):
-        here = pl.ds(pl.multiple_of(first, 16), rows)
-
-        @pl.when(blk != z)
+    lanes = pl.ds(0, 128)
+
+    def unit(half, first, rows, u, loads):
+        here = pl.ds(first, rows)
+
+        def body(n, scales):
+            if loads:
+                w_copy(n).wait()
+            lhs = jnp.concatenate([h[2 * half, here], h[2 * half + 1, here]], axis=0)
+            x = jnp.dot(lhs, w[n], preferred_element_type=jnp.float32)
+            cols = pl.ds(pl.multiple_of(n * tile, tile), tile)
+            out = []
+            for j in range(2):
+                blk = 2 * half + j
+                xj = x[j * rows:(j + 1) * rows]
+                coded, sc = code(xj, n, scales[j])
+                out.append(sc)
+
+                @pl.when(blk == z)
+                def _():
+                    acc[here, cols] = xj
+
+                @pl.when(z == inner(half))
+                def _():
+                    stash[j, here, cols] = xj
+
+                @pl.when(jnp.logical_and(blk != z, z != inner(half)))
+                def _():
+                    q_send[blk, here, cols] = coded
+                    post(blk, half, j, u, here, cols, False)
+            return tuple(out)
+
+        zero = jnp.zeros((rows, 128), jnp.float32)
+        scales = lax.fori_loop(0, TILES, body, (zero, zero))
+        for j in range(2):
+            blk = 2 * half + j
+
+            @pl.when(jnp.logical_and(blk != z, z != inner(half)))
+            def _():
+                s_send[blk, here] = scales[j].astype(jnp.bfloat16)
+                post(blk, half, j, u, here, lanes, True)
+
+    def merge(half, first, rows, u):
+        here = pl.ds(first, rows)
+
+        @pl.when(z == inner(half))
         def _():
-            s_send[blk, here] = scales.astype(jnp.bfloat16)
             remote(
-                s_send.at[blk, here], s_recv.at[z, here],
-                s_send_sem.at[blk], s_recv_sem.at[z], p, blk,
-            ).start()
+                m_recv.at[:, here], m_recv.at[:, here], q_send_sem.at[0], m_recv_sem.at[u], p, z
+            ).wait_recv()
+            remote(
+                ms_recv.at[:, here], ms_recv.at[:, here], s_send_sem.at[0], ms_recv_sem.at[u], p, z
+            ).wait_recv()
+            scales = [jnp.zeros((rows, 128), jnp.float32)] * 2
+            for n in range(TILES):
+                cols = pl.ds(n * tile, tile)
+                for j in range(2):
+                    blk = 2 * half + j
+                    x = stash[j, here, cols] + decode(m_recv[j, here, cols], ms_recv[j, here], n)
+                    coded, scales[j] = code(x, n, scales[j])
+                    q_send[blk, here, cols] = coded
+                    remote(
+                        q_send.at[blk, here, cols], q_recv.at[1, here, cols],
+                        q_send_sem.at[blk], q_recv_sem.at[1], p, blk,
+                    ).start()
+            for j in range(2):
+                blk = 2 * half + j
+                s_send[blk, here] = scales[j].astype(jnp.bfloat16)
+                remote(
+                    s_send.at[blk, here], s_recv.at[1, here],
+                    s_send_sem.at[blk], s_recv_sem.at[1], p, blk,
+                ).start()
 
     def slots_of(blk):
         per = block // SEGMENT_ROWS
@@ -195,19 +271,21 @@
         hidden_ref, h.at[core_peer], c_send_sem.at[0], c_recv_sem.at[0], core_peer, z
     ).wait_recv()
 
-    def near(n, scales):
-        w_copy(n).wait()
-        lhs = jnp.concatenate([h[y * 2], h[y * 2 + 1]], axis=0)
-        x = jnp.dot(lhs, w[n], preferred_element_type=jnp.float32)
-        return tuple(
-            emit(x[j * block:(j + 1) * block], n, y * 2 + j, 0, block, scales[j]) for j in range(2)
-        )
-
-    zero = jnp.zeros((block, 128), jnp.float32)
-    scales = lax.fori_loop(0, TILES, near, (zero, zero))
-    for j in range(2):
-        emit_scales(scales[j], y * 2 + j, 0, block)
-
+    near, far = [], []
+    for sizes, units in ((NEAR, near), (FAR, far)):
+        start = 0
+        for size in sizes:
+            units.append((start * part, size * part))
+            start += size
+
+    def near_merge(i):
+        merge(y, *near[i], i)
+
+    def far_merge(i):
+        merge(1 - y, *far[i], len(near) + i)
+
+    for i, rows in enumerate(near):
+        unit(y, *rows, i, i == 0)
     a_load.wait()
 
     def near_shrink(j, _):
@@ -216,35 +294,25 @@
 
     lax.fori_loop(0, 2, near_shrink, 0)
 
-    def far(k, _):
-        y_copy(k, y_peer).wait_recv()
-        fwd_copy(k, y_peer).start()
-        far_first = (1 - y) * 2
-        fwd_copy(k, far_first + (1 - c)).wait_recv()
-        first = pl.multiple_of(k * part, part)
-        rows = pl.ds(first, part)
-
-        def body(n, scales):
-            lhs = jnp.concatenate([h[far_first, rows], h[far_first + 1, rows]], axis=0)
-            x = jnp.dot(lhs, w[n], preferred_element_type=jnp.float32)
-            return tuple(
-                emit(x[j * part:(j + 1) * part], n, far_first + j, first, part, scales[j])
-                for j in range(2)
-            )
-
-        zero = jnp.zeros((part, 128), jnp.float32)
-        scales = lax.fori_loop(0, TILES, body, (zero, zero))
-        for j in range(2):
-            emit_scales(scales[j], far_first + j, first, part)
-        return 0
-
-    lax.fori_loop(0, CHUNKS, far, 0)
+    for i, (first, rows) in enumerate(far):
+        pieces = range(first // part, (first + rows) // part)
+        for k in pieces:
+            y_copy(k, y_peer).wait_recv()
+            fwd_copy(k, y_peer).start()
+        for k in pieces:
+            fwd_copy(k, (1 - y) * 2 + (1 - c)).wait_recv()
+        unit(1 - y, first, rows, len(near) + i, False)
+        if i < len(near):
+            near_merge(i)
+        if i >= 1:
+            far_merge(i - 1)
 
     def far_shrink(j, _):
         shrink_block((1 - y) * 2 + j)
         return 0
 
     lax.fori_loop(0, 2, far_shrink, 0)
+    far_merge(len(far) - 1)
 
     me = p * steps + z
     e_load.wait()
@@ -277,8 +345,7 @@
     live = jnp.zeros((block, 1), jnp.int32)
     for i in range(per):
         live = jnp.where(row >= i * SEGMENT_ROWS, count_ref[z * per + i] + i * SEGMENT_ROWS, live)
-    for i in range(1, steps):
-        src = (z + i) % steps
+    for src in range(2):
         remote(
             q_recv.at[src], q_recv.at[src], q_send_sem.at[src], q_recv_sem.at[src], p, z
         ).wait_recv()
@@ -288,23 +355,21 @@
     for n in range(TILES):
         cols = slice(n * tile, (n + 1) * tile)
         x = acc[:, cols]
-        for i in range(1, steps):
-            src = (z + i) % steps
-            scale = s_recv[src].astype(jnp.float32)[:, n:n + 1]
-            x = x + q_recv[src, :, cols].astype(jnp.int32).astype(jnp.float32) * scale
+        for src in range(2):
+            x = x + decode(q_recv[src, :, cols], s_recv[src], n)
         out_ref[:, cols] = jnp.where(row < live, x, 0.0).astype(jnp.bfloat16)
 
     core_copy(p).wait_send()
-    for k in range(CHUNKS):
+    for k in range(PIECES):
         y_copy(k, p).wait_send()
         fwd_copy(k, y_peer).wait_send()
     for i in range(1, steps):
         blk = (z + i) % steps
         remote(
-            q_send.at[blk], q_recv.at[z], q_send_sem.at[blk], q_recv_sem.at[z], p, blk
+            q_send.at[blk], q_recv.at[0], q_send_sem.at[blk], q_recv_sem.at[0], p, blk
         ).wait_send()
         remote(
-            s_send.at[blk], s_recv.at[z], s_send_sem.at[blk], s_recv_sem.at[z], p, blk
+            s_send.at[blk], s_recv.at[0], s_send_sem.at[blk], s_recv_sem.at[0], p, blk
         ).wait_send()
     for t in range(steps):
         for i in range(pools):
@@ -347,15 +412,18 @@
             pltpu.VMEM((owned * rank, ff), bf16),
             pltpu.VMEM((adapters * rank, width), bf16),
             pltpu.VMEM((block, width), f32),
+            pltpu.VMEM((2, block, width), f32),
             pltpu.VMEM((steps, block, width), jnp.int16),
-            pltpu.VMEM((steps, block, width), jnp.int16),
+            pltpu.VMEM((2, block, width), jnp.int16),
             pltpu.VMEM((steps, block, 128), bf16),
-            pltpu.VMEM((steps, block, 128), bf16),
+            pltpu.VMEM((2, block, 128), bf16),
+            pltpu.VMEM((2, block, width), jnp.int16),
+            pltpu.VMEM((2, block, 128), bf16),
             pltpu.VMEM((steps, rank, block), f32),
             pltpu.VMEM((pools * steps, rank, block), f32),
-            dma((TILES,)), dma((3,)), dma((CHUNKS,)), dma((CHUNKS,)), dma((1,)), dma((1,)),
-            dma((CHUNKS,)), dma((CHUNKS,)), dma((steps,)), dma((steps,)), dma((steps,)),
-            dma((steps,)), dma((pools * steps,)), dma((pools * steps,)),
+            dma((TILES,)), dma((3,)), dma((PIECES,)), dma((PIECES,)), dma((1,)), dma((1,)),
+            dma((PIECES,)), dma((PIECES,)), dma((steps,)), dma((2,)), dma((steps,)), dma((2,)),
+            dma((len(NEAR + FAR),)), dma((len(NEAR + FAR),)), dma((pools * steps,)), dma((pools * steps,)),
         ],
         compiler_params=pltpu.CompilerParams(
             collective_id=0, has_side_effects=True, vmem_limit_bytes=VMEM_LIMIT

time: 84.4 us -> 76.7 us (0.909); the launches traced: 84.3 us -> 75.3 us
  Pallas kernels: 82.4 us -> 73.4 us
    pallas_call x1, Pallas kernels: 82.4 us -> 73.4 us  [fused_device(): pl.pallas_call(fused_kernel, out_shape=jax.ShapeDtypeStruct((block, width...]
where the time goes in v2:
time: 76.7 us; the launch traced here: 75.3 us
  Pallas kernels  73.4 us (96%)
  local copies, waits for them, and re-layouts  1.88 us (2%)
    pallas_call x1, Pallas kernels, fused_device(): pl.pallas_call(fused_kernel, out_shape=jax.ShapeDtypeStruct((block, width...  73.4 us
    unnamed x1, local copies, waits for them, and re-layouts  1.88 us

profile of v2, /device:TPU:0, one launch (start us, length us, event | category | flops | bytes accessed | tf_op | source)
XLA Modules:
  0.0 75.3 jit_solution(13154401124594879837)
XLA Ops:
  0.0 73.4 %shard_map.73 = bf16[128,2048]{1,0:T(8,128)(2,1)} custom-call(s32[32]{0:T(128)} %id_ref.1, s32[16]{0:T(128)} %slot_ref.1, s32[32]{0:T(128)} %count_ref.1, bf16[128,7168]{1,0:T(8,128)(2,1)} %hidden_ref.1, bf16[7168,2048]{1,0:T(8,128)(2,1)} %down_ref.1, bf16[64,7168]{1,0:T(8,128)(2,1)} %bitcast.3, bf16[256,2048]{1,0:T(8,128)(2,1)} %bitcast.2), custom_call_target="tpu_custom_call" | custom-call | flops 15032385536 | bytes 29360128 | tf_op jit(solution)/shard_map/pallas_call | solution.py:404
  73.4 1.9 %copy.9 = bf16[128,2048]{1,0:T(8,128)(2,1)} copy(bf16[128,2048]{1,0:T(8,128)(2,1)} %shard_map.73) | data formatting | bytes 1048576

commit v3 on v2

--- a/solution.py
+++ b/solution.py
@@ -58,7 +58,7 @@
 TILES = 4
 VMEM_LIMIT = 60 * 2**20
 PIECES = 8
-NEAR = (4, 4)
+NEAR = (8,)
 FAR = (2, 3, 2, 1)
 
 

time: 76.7 us -> 75.7 us (0.987)
  no operation moved by 1% of the time
where the time goes in v3:
time: 75.7 us; the launch traced here: 74.6 us
  Pallas kernels  72.7 us (96%)
  local copies, waits for them, and re-layouts  1.88 us (2%)
    pallas_call x1, Pallas kernels, fused_device(): pl.pallas_call(fused_kernel, out_shape=jax.ShapeDtypeStruct((block, width...  72.7 us
    unnamed x1, local copies, waits for them, and re-layouts  1.88 us

profile of v3, /device:TPU:0, one launch (start us, length us, event | category | flops | bytes accessed | tf_op | source)
XLA Modules:
  0.0 74.6 jit_solution(2252489506730978583)
XLA Ops:
  0.0 72.7 %shard_map.73 = bf16[128,2048]{1,0:T(8,128)(2,1)} custom-call(s32[32]{0:T(128)} %id_ref.1, s32[16]{0:T(128)} %slot_ref.1, s32[32]{0:T(128)} %count_ref.1, bf16[128,7168]{1,0:T(8,128)(2,1)} %hidden_ref.1, bf16[7168,2048]{1,0:T(8,128)(2,1)} %down_ref.1, bf16[64,7168]{1,0:T(8,128)(2,1)} %bitcast.3, bf16[256,2048]{1,0:T(8,128)(2,1)} %bitcast.2), custom_call_target="tpu_custom_call" | custom-call | flops 15032385536 | bytes 29360128 | tf_op jit(solution)/shard_map/pallas_call | solution.py:404
  72.7 1.9 %copy.9 = bf16[128,2048]{1,0:T(8,128)(2,1)} copy(bf16[128,2048]{1,0:T(8,128)(2,1)} %shard_map.73) | data formatting | bytes 1048576
